TPU v7x, 512 devices: a whole 4x4x16 slice. The times are simulated.
512 devices in a mesh: row: 16 (over y, z_hi, core), col: 32 (over z_lo, x).
Axes of the slice: x: 4, y: 4, z: 16 (z_hi: 2, z_lo: 8; z = z_hi * 8 + z_lo), core: 2. Of those that a mesh axis runs over, the one named last changes fastest.
Arguments:
- features: bfloat16 [65536, 128], P(('col', 'row')), may hold values from -6 to 6
- weight: bfloat16 [128, 256], replicated, may hold values from -0.5 to 0.5
- tile_values: bfloat16 [16, 4096, 128, 128], P('row', 'col'), may hold values from -0.078125 to 0.078125
- tile_row: int32 [16, 4096], P('row', 'col'), may hold values from 0 to 31
- tile_col: int32 [16, 4096], P('row', 'col'), may hold values from 0 to 15
- tile_count: int32 [16, 32], P('row', 'col'), may hold values from 16 to 128, as said below
- upstream: bfloat16 [65536, 256], P(('row', 'col')), may hold values from -6 to 6
Outputs:
- activated: bfloat16 [65536, 256], P(('row', 'col'))
- feature_grad: bfloat16 [65536, 128], P(('col', 'row'))
- weight_grad: float32 [128, 256], replicated
Inputs may be any that keep to these rules, and one draw needn't show every extreme that they name: `tile_count`: some device has all 128 slots live.
All inputs are finite; a program needn't handle non-finite values.
Results may differ from a plain program's by a relative error of at most 0.03.
Values may be sent and summed in bfloat16 or wider, within the bound.
A program may use at most 64 MiB of HBM per device.

v0:
```python
import math

import jax
import jax.numpy as jnp
from jax import lax
from jax.sharding import PartitionSpec as P


def block_product(values, source_index, target_index, live_count, source, target_tiles, transpose):
    slots = values.shape[0]
    tile_size = values.shape[1]
    width = source.shape[2]
    block_size = math.gcd(slots, 32)
    blocks_used = (live_count + block_size - 1) // block_size
    offsets = jnp.arange(block_size, dtype=jnp.int32)

    def step(index, total):
        start = (index * block_size).astype(jnp.int32)
        block_values = lax.dynamic_slice_in_dim(values, start, block_size, 0)
        block_source = lax.dynamic_slice_in_dim(source_index, start, block_size, 0)
        block_target = lax.dynamic_slice_in_dim(target_index, start, block_size, 0)
        block_live = start + offsets < live_count
        picked = source[block_source]
        if transpose:
            product = jnp.einsum(
                "kjt,kjh->kth", block_values, picked, preferred_element_type=jnp.float32
            )
        else:
            product = jnp.einsum(
                "ktj,kjh->kth", block_values, picked, preferred_element_type=jnp.float32
            )
        product = jnp.where(block_live[:, None, None], product, 0.0)
        return total.at[block_target].add(product)

    total = lax.fori_loop(
        0, blocks_used, step, jnp.zeros((target_tiles, tile_size, width), jnp.float32)
    )
    return total.reshape(target_tiles * tile_size, width)


def per_device(features, weight, tile_values, tile_row, tile_col, tile_count, upstream):
    rows_here = features.shape[0]
    in_width = features.shape[1]
    tile_size = tile_values.shape[2]
    count_row = lax.axis_size("row")
    count_col = lax.axis_size("col")
    values = tile_values[0]
    rows_here_tiles = tile_row[0]
    cols_here_tiles = tile_col[0]
    live_count = tile_count[0, 0]
    source = lax.all_gather(features, "row", axis=0, tiled=True)
    source = source.reshape(source.shape[0] // tile_size, tile_size, in_width)
    row_tiles = rows_here * count_col // tile_size
    col_tiles = rows_here * count_row // tile_size
    partial_value = block_product(
        values, cols_here_tiles, rows_here_tiles, live_count, source, row_tiles, False
    )
    aggregated = lax.psum_scatter(
        partial_value.astype(jnp.bfloat16), "col", scatter_dimension=0, tiled=True
    )
    summed = jnp.dot(aggregated, weight, preferred_element_type=jnp.float32)
    sigma = jax.nn.sigmoid(summed)
    activated = (summed * sigma).astype(jnp.bfloat16)
    slope = sigma * (1.0 + summed * (1.0 - sigma))
    grad_rows = (upstream.astype(jnp.float32) * slope).astype(jnp.bfloat16)
    weight_term = jnp.dot(aggregated.T, grad_rows, preferred_element_type=jnp.float32)
    back_local = jnp.dot(grad_rows, weight.T, preferred_element_type=jnp.float32).astype(
        jnp.bfloat16
    )
    gathered_back = lax.all_gather(back_local, "col", axis=0, tiled=True)
    grad_source = gathered_back.reshape(row_tiles, tile_size, in_width)
    back_partial = block_product(
        values, rows_here_tiles, cols_here_tiles, live_count, grad_source, col_tiles, True
    )
    feature_grad = lax.psum_scatter(
        back_partial.astype(jnp.bfloat16), "row", scatter_dimension=0, tiled=True
    )
    nodes_total = rows_here * count_row * count_col
    weight_grad = lax.psum(weight_term, ("row", "col")) * (1.0 / math.sqrt(nodes_total))
    return (activated, feature_grad, weight_grad)


def solution(mesh):
    in_specs = (
        P(("col", "row"), None),
        P(),
        P("row", "col", None, None),
        P("row", "col"),
        P("row", "col"),
        P("row", "col"),
        P(("row", "col"), None),
    )
    out_specs = (P(("row", "col"), None), P(("col", "row"), None), P())
    return jax.shard_map(
        per_device, mesh=mesh, in_specs=in_specs, out_specs=out_specs, check_vma=False
    )
```

profile of v0, /device:TPU:1, one launch (start us, length us, event | category | flops | bytes accessed | tf_op | source)
XLA Modules:
  0.0 1120.8 jit_solution(8585932190667194005)
XLA Ops:
  7.2 0.0 reduce-scatter.3.cloned.1.call-start
  7.9 63.2 %all_gather.6 = bf16[2048,128]{1,0:T(8,128)(2,1)} all-gather(bf16[128,128]{1,0:T(8,128)(2,1)} %param.11), channel_id=1, replica_groups=mesh['row'=16,'col'=32] {'row'}, dimensions={0}, use_global_device_ids=true | all-gather | bytes 557056 | tf_op jit(solution)/shard_map/all_gather | solution.py:51
  71.1 1.6 broadcast_in_dim.40
  72.7 10.4 while.22
  72.7 0.1 compare_select_fusion.6
  72.8 1.8 gather_fusion
  74.6 0.7 fusion.27
  75.3 1.7 convolution_select_fusion.4
  76.9 6.2 scatter_fusion
  83.1 2.8 convert_element_type.24
  85.9 0.0 reduce-scatter.3.cloned.1.call-update
  85.9 0.0 all-gather.2.cloned.1.call-start
  86.0 238.9 %reduce-scatter.3.cloned.1.call-done = bf16[128,128]{1,0:T(8,128)(2,1)} async-done(((bf16[4096,128]{1,0:T(8,128)(2,1)}), bf16[128,128]{1,0:T(8,128)(2,1)}) %reduce-scatter.3.cloned.1.call-update) | async-done | bytes 32784 | tf_op jit(solution)/shard_map/reduce_scatter | solution.py:58
  324.9 1.6 multiply_convert_fusion
  326.5 0.8 convolution_convert_fusion
  327.2 0.0 all-gather.2.cloned.1.call-update
  327.3 0.0 all-reduce.2.cloned.1.call-start
  327.3 6.4 copy.10
  333.7 0.9 fusion.10
  334.6 0.0 reduce-scatter.5.cloned.1.call-start
  334.6 210.4 %all-gather.2.cloned.1.call-done = bf16[4096,128]{1,0:T(8,128)(2,1)} async-done(((bf16[128,128]{1,0:T(8,128)(2,1)}), bf16[4096,128]{1,0:T(8,128)(2,1)}) %all-gather.2.cloned.1.call-update) | async-done | bytes 1048592 | tf_op jit(solution)/shard_map/all_gather | solution.py:70
  545.0 0.1 broadcast_in_dim.41
  545.1 8.3 while.23
  545.1 0.1 compare_select_fusion.7
  545.2 2.9 gather_fusion.1
  548.1 0.7 fusion.30
  548.8 2.0 convolution_select_fusion.5
  550.8 2.7 scatter_fusion.1
  553.5 0.9 convert_element_type.30
  554.4 465.6 %all-reduce.2.cloned.1.call-done = f32[128,256]{1,0:T(8,128)} async-done(((f32[128,256]{1,0:T(8,128)}), f32[128,256]{1,0:T(8,128)}) %all-reduce.2.cloned.1.call-update) | async-done | bytes 131088 | tf_op jit(solution)/shard_map/psum | solution.py:79
  1019.9 1.6 broadcast_multiply_fusion
  1021.5 92.7 %reduce-scatter.5.cloned.1.call-done = bf16[128,128]{1,0:T(8,128)(2,1)} async-done(((bf16[2048,128]{1,0:T(8,128)(2,1)}), bf16[128,128]{1,0:T(8,128)(2,1)}) %reduce-scatter.5.cloned.1.call-update) | async-done | bytes 32784 | tf_op jit(solution)/shard_map/reduce_scatter | solution.py:75
  (14 shorter events, 0.1 us)
Async XLA Ops:
  7.2 317.7 %copy-start = (bf16[128,256]{1,0:T(8,128)(2,1)S(1)}, bf16[128,256]{1,0:T(8,128)(2,1)}, u32[]{:S(2)}) copy-start(bf16[128,256]{1,0:T(8,128)(2,1)} %param.12) | copy-start | bytes 196612
  7.2 65.5 %copy-start.1 = (s32[1,128]{1,0:T(1,128)S(1)}, s32[1,128]{1,0:T(1,128)}, u32[]{:S(2)}) copy-start(s32[1,128]{1,0:T(1,128)} %param.14) | copy-start | bytes 1540
  7.2 65.5 %copy-start.2 = (s32[1,128]{1,0:T(1,128)S(1)}, s32[1,128]{1,0:T(1,128)}, u32[]{:S(2)}) copy-start(s32[1,128]{1,0:T(1,128)} %param.15) | copy-start | bytes 1540
  7.2 317.7 %reduce-scatter.3.cloned.1.call-start = ((), (), s32[]{:S(2)}) async-start(), calls=%async_computation.2 | async-start | bytes 1081344 | tf_op jit(solution)/shard_map/reduce_scatter | solution.py:58
  83.1 241.8 %copy-start.4 = (bf16[128,256]{1,0:T(8,128)(2,1)S(1)}, bf16[128,256]{1,0:T(8,128)(2,1)}, u32[]{:S(2)}) copy-start(bf16[128,256]{1,0:T(8,128)(2,1)} %param.17) | copy-start | bytes 196612
  85.9 459.1 %all-gather.2.cloned.1.call-start = ((), (), s32[]{:S(2)}) async-start(), calls=%async_computation.3 | async-start | bytes 1081344 | tf_op jit(solution)/shard_map/all_gather | solution.py:70
  327.3 692.7 %all-reduce.2.cloned.1.call-start = ((), (), s32[]{:S(2)}) async-start(), calls=%async_computation.5 | async-start | bytes 262144 | tf_op jit(solution)/shard_map/psum | solution.py:79
  327.3 6.4 copy-start.3
  334.6 779.7 %reduce-scatter.5.cloned.1.call-start = ((), (), s32[]{:S(2)}) async-start(), calls=%async_computation.4 | async-start | bytes 557056 | tf_op jit(solution)/shard_map/reduce_scatter | solution.py:75
Sparse Core Ops, SparseCore 0:
  86.0 238.7 reduce-scatter.2
  327.7 217.2 all-gather.1
  551.9 467.9 all-reduce.1
  1025.0 89.1 reduce-scatter.4
where the time goes:
time: 1120 us
  waiting for transfers between devices  1010 us (90%)
  blocking collectives  63.2 us (6%)
  other arithmetic  15.5 us (1%)
  between operations  14.5 us (1%)
  local copies, waits for them, and re-layouts  12.8 us (1%)
    psum x1, waiting for transfers between devices, per_device(): lax.psum(weight_term, ('row', 'col')) * (1.0 / math.sqrt(nodes_total))  466 us
    reduce_scatter x1, waiting for transfers between devices, per_device(): lax.psum_scatter(partial_value.astype(jnp.bfloat16), 'col', scatter_dimen...  239 us
    all_gather x1, waiting for transfers between devices, per_device(): gathered_back = lax.all_gather(back_local, 'col', axis=0, tiled=True)  210 us
    reduce_scatter x1, waiting for transfers between devices, per_device(): lax.psum_scatter(back_partial.astype(jnp.bfloat16), 'row', scatter_dimens...  92.7 us
    all_gather x1, blocking collectives, per_device(): source = lax.all_gather(features, 'row', axis=0, tiled=True)  63.2 us
  transfers between devices with their start and end apart: 4, of which 4 were waited for; matrix products, arithmetic and copies ran while one was open for 2% of the time, Pallas kernels for 0%

commit v1 on v0

v1 whole, which is shorter than its diff:
```python
import functools
import math

import jax
import jax.numpy as jnp
from jax import lax
from jax.experimental import pallas as pl
from jax.experimental.pallas import tpu as pltpu
from jax.sharding import PartitionSpec as P

MESH = pl.DeviceIdType.MESH
F32 = jnp.float32
BF16 = jnp.bfloat16
T = 128

NX, NZ, NY, NH, NC = 4, 8, 4, 2, 2


def order_tables(target, source, live, bins):
    slots = target.shape[1]
    lane = lax.broadcasted_iota(jnp.int32, (slots, slots), 1)
    sub = lax.broadcasted_iota(jnp.int32, (slots, slots), 0)
    wide = jnp.where(lane < live, jnp.broadcast_to(target, (slots, slots)), bins)
    key = wide * slots + lane
    tall = wide.T
    tall_key = tall * slots + sub
    rank = jnp.sum((tall_key < key).astype(jnp.int32), axis=0, keepdims=True)
    tall_rank = jnp.broadcast_to(rank, (slots, slots)).T
    placed = tall_rank == lane
    tall_source = jnp.broadcast_to(source, (slots, slots)).T
    perm = jnp.sum(jnp.where(placed, sub, 0), axis=0, keepdims=True)
    src = jnp.sum(jnp.where(placed, tall_source, 0), axis=0, keepdims=True)
    place = jnp.sum(jnp.where(placed, tall, 0), axis=0, keepdims=True)
    before = jnp.sum(jnp.where(tall_rank + 1 == lane, tall, 0), axis=0, keepdims=True)
    first = lax.broadcasted_iota(jnp.int32, (1, slots), 1) == 0
    keep = jnp.where((place == before) & jnp.logical_not(first), 1, 0)
    upto = jnp.sum((tall <= lane).astype(jnp.int32), axis=0, keepdims=True)
    here = jnp.sum((tall == lane).astype(jnp.int32), axis=0, keepdims=True)
    last = jnp.where(here > 0, upto - 1, slots)
    return perm, src, keep, last


def kernel(
    scale,
    feat_ref, weight_ref, vals_hbm, row_ref, col_ref, count_ref, up_ref,
    act_ref, fg_ref, wg_ref,
    vals, xbuf, sums, pbuf, rx, zs, rz, bbuf, qpack, rq, ys, ry, zh, rzh,
    wown, rw1, ws2, rw2, ws3, rw3, ws4, rw4, ws5, rw5, wy, wall,
    tabv, tabs,
    local_sem, x_send, x_recv, px_send, px_recv, pz_send, pz_recv, b_send, b_recv,
    qc_send, qc_recv, qy_send, qy_recv, qh_send, qh_recv, w_send, w_recv,
):
    r = lax.axis_index("row")
    c = lax.axis_index("col")
    y, h, core = r // (NH * NC), (r // NC) % NH, r % NC
    z, x = c // NX, c % NX
    slots = vals.shape[0]
    sent = []

    def rowdev(yy, hh, cc):
        return {"row": (yy * NH + hh) * NC + cc, "col": c}

    def coldev(zz, xx):
        return {"row": r, "col": zz * NX + xx}

    def send(src, dst, send_sem, recv_sem, device):
        copy = pltpu.make_async_remote_copy(
            src_ref=src, dst_ref=dst, send_sem=send_sem, recv_sem=recv_sem, device_id=device, device_id_type=MESH
        )
        copy.start()
        sent.append(copy)

    def arrived(dst, recv_sem):
        pltpu.make_async_remote_copy(
            src_ref=dst, dst_ref=dst, send_sem=recv_sem, recv_sem=recv_sem, device_id=rowdev(y, h, 1 - core), device_id_type=MESH
        ).wait_recv()

    barrier = pltpu.get_barrier_semaphore()
    peers = [rowdev(y, h, 1 - core), rowdev(y, 1 - h, core)]
    peers += [rowdev((y + d) % NY, h, core) for d in range(1, NY)]
    peers += [coldev(z, (x + d) % NX) for d in range(1, NX)]
    peers += [coldev((z + d) % NZ, x) for d in range(1, NZ)]
    for peer in peers:
        pl.semaphore_signal(barrier, inc=1, device_id=peer, device_id_type=MESH)
    vals_copy = pltpu.make_async_copy(vals_hbm.at[0], vals, local_sem.at[0])
    vals_copy.start()
    live = count_ref[0, 0]
    forward = order_tables(row_ref[...], col_ref[...], live, NZ * NX)
    for i, table in enumerate(forward):
        tabv[i : i + 1, :] = table
    backward = order_tables(col_ref[...], row_ref[...], live, NY * NH * NC)
    for i, table in enumerate(backward):
        tabv[4 + i : 5 + i, :] = table
    tabs_copy = pltpu.make_async_copy(tabv, tabs, local_sem.at[1])
    tabs_copy.start()
    sums[slots] = jnp.zeros((T, T), BF16)
    xbuf[r] = feat_ref[...]
    pl.semaphore_wait(barrier, len(peers))

    def tile_of(yy, hh, cc):
        return (yy * NH + hh) * NC + cc

    n = [0]

    def share(tile, device):
        send(xbuf.at[tile], xbuf.at[tile], x_send.at[n[0]], x_recv.at[tile], device)
        n[0] += 1

    share(r, rowdev(y, 1 - h, core))
    for d in range(1, NY):
        share(r, rowdev((y + d) % NY, h, core))
    share(r, rowdev(y, h, 1 - core))
    other = tile_of(y, 1 - h, core)
    arrived(xbuf.at[other], x_recv.at[other])
    for d in range(1, NY):
        share(other, rowdev((y + d) % NY, h, core))
    share(other, rowdev(y, h, 1 - core))
    for hh in (h, 1 - h):
        for d in range(1, NY):
            tile = tile_of((y + d) % NY, hh, core)
            arrived(xbuf.at[tile], x_recv.at[tile])
            share(tile, rowdev(y, h, 1 - core))
    for hh in range(NH):
        for yy in range(NY):
            tile = tile_of(yy, hh, 1 - core)
            arrived(xbuf.at[tile], x_recv.at[tile])

    tabs_copy.wait()
    vals_copy.wait()

    def product_scan(base, multiply):
        def body(step, total):
            for u in range(8):
                k = step * 8 + u
                keep = tabs[base + 2, k].astype(F32)
                total = total * keep + multiply(tabs[base, k], tabs[base + 1, k])
                sums[k] = total.astype(BF16)
            return total

        lax.fori_loop(0, slots // 8, body, jnp.zeros((T, T), F32))

    product_scan(0, lambda i, s: jnp.dot(vals[i], xbuf[s], preferred_element_type=F32))

    for o in range(1, NZ + 1):
        zz = (z + o) % NZ
        for xx in range(NX):
            pbuf[xx, zz] = sums[tabs[3, zz * NX + xx]]
        for d in range(1, NX):
            send(
                pbuf.at[(x + d) % NX, zz], rx.at[d - 1, o - 1],
                px_send.at[d - 1, o - 1], px_recv.at[d - 1, o - 1], coldev(z, (x + d) % NX),
            )
    for o in range(1, NZ + 1):
        zz = (z + o) % NZ
        total = pbuf[x, zz].astype(F32)
        for d in range(1, NX):
            arrived(rx.at[d - 1, o - 1], px_recv.at[d - 1, o - 1])
            total += rx[d - 1, o - 1].astype(F32)
        if o < NZ:
            zs[o - 1] = total.astype(BF16)
            send(zs.at[o - 1], rz.at[o - 1], pz_send.at[o - 1], pz_recv.at[o - 1], coldev(zz, x))
    for o in range(1, NZ):
        arrived(rz.at[o - 1], pz_recv.at[o - 1])
        total += rz[o - 1].astype(F32)
    aggregated = total.astype(BF16)

    weight = weight_ref[...]
    summed = jnp.dot(aggregated, weight, preferred_element_type=F32)
    sigma = jax.nn.sigmoid(summed)
    slope = sigma * (1.0 + summed * (1.0 - sigma))
    grad_rows = (up_ref[...].astype(F32) * slope).astype(BF16)
    back = lax.dot_general(weight, grad_rows, (((1,), (1,)), ((), ())), preferred_element_type=F32)
    bbuf[c] = back.astype(BF16)

    for o in range(1, NZ):
        send(bbuf.at[c], bbuf.at[c], b_send.at[0, o - 1], b_recv.at[c], coldev((z + o) % NZ, x))
    for d in range(1, NX):
        send(bbuf.at[c], bbuf.at[c], b_send.at[d, 0], b_recv.at[c], coldev(z, (x + d) % NX))
    act_ref[...] = (summed * sigma).astype(BF16)
    wown[...] = jnp.dot(aggregated.astype(F32).T.astype(BF16), grad_rows, preferred_element_type=F32)
    wx = wown.shape[0] // NX
    wyn = wx // NY
    m = [0]

    def wsend(src, dst, slot, device):
        send(src, dst, w_send.at[m[0]], w_recv.at[slot], device)
        m[0] += 1

    for d in range(1, NX):
        wsend(wown.at[pl.ds(((x + d) % NX) * wx, wx)], rw1.at[d - 1], d - 1, coldev(z, (x + d) % NX))
    for o in range(1, NZ):
        t = ((z + NZ - o) % NZ) * NX + x
        arrived(bbuf.at[t], b_recv.at[t])
        for d in range(1, NX):
            send(bbuf.at[t], bbuf.at[t], b_send.at[d, o], b_recv.at[t], coldev(z, (x + d) % NX))
    total = wown[pl.ds(x * wx, wx), :]
    for d in range(1, NX):
        arrived(rw1.at[d - 1], w_recv.at[d - 1])
        total += rw1[d - 1]
    ws2[...] = total
    base = NX - 1
    for d in range(1, NY):
        wsend(ws2.at[pl.ds(((y + d) % NY) * wyn, wyn)], rw2.at[d - 1], base + d - 1, rowdev((y + d) % NY, h, core))
    for o in range(NZ):
        for d in range(1, NX):
            t = ((z + NZ - o) % NZ) * NX + (x + d) % NX
            arrived(bbuf.at[t], b_recv.at[t])
    total = ws2[pl.ds(y * wyn, wyn), :]
    for d in range(1, NY):
        arrived(rw2.at[d - 1], w_recv.at[base + d - 1])
        total += rw2[d - 1]
    base += NY - 1
    ws3[...] = total
    wsend(ws3, rw3, base, rowdev(y, h, 1 - core))

    product_scan(4, lambda i, s: jnp.dot(bbuf[s], vals[i], preferred_element_type=F32))

    for o in range(1, NY + 1):
        yy = (y + o) % NY
        for cc in range(NC):
            for hh in range(NH):
                qpack[cc, yy, hh] = sums[tabs[7, tile_of(yy, hh, cc)]]
        send(
            qpack.at[1 - core, yy], rq.at[yy], qc_send.at[o - 1], qc_recv.at[yy], rowdev(y, h, 1 - core)
        )
    arrived(rw3, w_recv.at[base])
    total = ws3[...] + rw3[...]
    ws4[...] = total
    base += 1
    for o in range(1, NZ):
        wsend(ws4, rw4.at[o - 1], base + o - 1, coldev((z + o) % NZ, x))
    for o in range(1, NY + 1):
        yy = (y + o) % NY
        arrived(rq.at[yy], qc_recv.at[yy])
        pair = qpack[core, yy].astype(F32) + rq[yy].astype(F32)
        if o < NY:
            ys[o - 1] = pair.astype(BF16)
            send(ys.at[o - 1], ry.at[o - 1], qy_send.at[o - 1], qy_recv.at[o - 1], rowdev(yy, h, core))
        else:
            ys[o - 1] = pair.astype(BF16)
    for o in range(1, NZ):
        arrived(rw4.at[o - 1], w_recv.at[base + o - 1])
        total += rw4[o - 1]
    base += NZ - 1
    ws5[...] = total
    wsend(ws5, rw5, base, rowdev(y, 1 - h, core))
    for o in range(1, NY):
        arrived(ry.at[o - 1], qy_recv.at[o - 1])
    away = ys[NY - 1, 1 - h].astype(F32)
    mine = ys[NY - 1, h].astype(F32)
    for o in range(1, NY):
        away += ry[o - 1, 1 - h].astype(F32)
    zh[...] = away.astype(BF16)
    send(zh, rzh, qh_send, qh_recv, rowdev(y, 1 - h, core))
    for o in range(1, NY):
        mine += ry[o - 1, h].astype(F32)
    arrived(rw5, w_recv.at[base])
    base += 1
    wy[pl.ds(y * wyn, wyn), :] = (ws5[...] + rw5[...]) * scale
    piece = wy.at[pl.ds(y * wyn, wyn)]
    for d in range(1, NY):
        wsend(piece, piece, base + d - 1, rowdev((y + d) % NY, h, core))
    for d in range(1, NY):
        arrived(wy.at[pl.ds(((y + NY - d) % NY) * wyn, wyn)], w_recv.at[base + d - 1])
    base += NY - 1
    wall[pl.ds(x * wx, wx), :] = wy[...]
    piece = wall.at[pl.ds(x * wx, wx)]
    for d in range(1, NX):
        wsend(piece, piece, base + d - 1, coldev(z, (x + d) % NX))
    arrived(rzh, qh_recv)
    fg_ref[...] = (mine + rzh[...].astype(F32)).T.astype(BF16)
    for d in range(1, NX):
        arrived(wall.at[pl.ds(((x + NX - d) % NX) * wx, wx)], w_recv.at[base + d - 1])
    wg_ref[...] = wall[...]
    for copy in sent:
        copy.wait_send()


def per_device(features, weight, tile_values, tile_row, tile_col, tile_count, upstream):
    rows, width = features.shape
    hidden = weight.shape[1]
    slots = tile_values.shape[1]
    nodes = rows * lax.axis_size("row") * lax.axis_size("col")
    tile = (T, T)
    wx = width // NX
    wyn = wx // NY
    dma = pltpu.SemaphoreType.DMA
    vm = pl.BlockSpec(memory_space=pltpu.VMEM)
    w_count = (NX - 1) + (NY - 1) + 1 + (NZ - 1) + 1 + (NY - 1) + (NX - 1)
    flops = 2 * 2 * slots * T * T * T
    return pl.pallas_call(
        functools.partial(kernel, 1.0 / math.sqrt(nodes)),
        out_shape=(
            jax.ShapeDtypeStruct((rows, hidden), BF16),
            jax.ShapeDtypeStruct((rows, width), BF16),
            jax.ShapeDtypeStruct((width, hidden), F32),
        ),
        in_specs=[
            vm, vm, pl.BlockSpec(memory_space=pl.ANY), vm, vm, pl.BlockSpec(memory_space=pltpu.SMEM), vm,
        ],
        out_specs=(vm, vm, vm),
        scratch_shapes=[
            pltpu.VMEM((slots,) + tile, BF16),
            pltpu.VMEM((NY * NH * NC,) + tile, BF16),
            pltpu.VMEM((slots + 1,) + tile, BF16),
            pltpu.VMEM((NX, NZ) + tile, BF16),
            pltpu.VMEM((NX - 1, NZ) + tile, BF16),
            pltpu.VMEM((NZ - 1,) + tile, BF16),
            pltpu.VMEM((NZ - 1,) + tile, BF16),
            pltpu.VMEM((NZ * NX,) + tile, BF16),
            pltpu.VMEM((NC, NY, NH) + tile, BF16),
            pltpu.VMEM((NY, NH) + tile, BF16),
            pltpu.VMEM((NY, NH) + tile, BF16),
            pltpu.VMEM((max(NY - 1, 1), NH) + tile, BF16),
            pltpu.VMEM(tile, BF16),
            pltpu.VMEM(tile, BF16),
            pltpu.VMEM((width, hidden), F32),
            pltpu.VMEM((NX - 1, wx, hidden), F32),
            pltpu.VMEM((wx, hidden), F32),
            pltpu.VMEM((max(NY - 1, 1), wyn, hidden), F32),
            pltpu.VMEM((wyn, hidden), F32),
            pltpu.VMEM((wyn, hidden), F32),
            pltpu.VMEM((wyn, hidden), F32),
            pltpu.VMEM((NZ - 1, wyn, hidden), F32),
            pltpu.VMEM((wyn, hidden), F32),
            pltpu.VMEM((wyn, hidden), F32),
            pltpu.VMEM((wx, hidden), F32),
            pltpu.VMEM((width, hidden), F32),
            pltpu.VMEM((8, slots), jnp.int32),
            pltpu.SMEM((8, slots), jnp.int32),
            dma((2,)),
            dma((NY * NH * NC,)), dma((NY * NH * NC,)),
            dma((NX - 1, NZ)), dma((NX - 1, NZ)),
            dma((NZ - 1,)), dma((NZ - 1,)),
            dma((NX, NZ)), dma((NZ * NX,)),
            dma((NY,)), dma((NY,)),
            dma((max(NY - 1, 1),)), dma((max(NY - 1, 1),)),
            dma, dma,
            dma((w_count,)), dma((w_count,)),
        ],
        compiler_params=pltpu.CompilerParams(
            collective_id=0, has_side_effects=True, vmem_limit_bytes=40 * 1024 * 1024
        ),
        cost_estimate=pl.CostEstimate(flops=flops, bytes_accessed=slots * T * T * 2, transcendentals=rows * hidden),
    )(features, weight, tile_values, tile_row, tile_col, tile_count, upstream)


def solution(mesh):
    in_specs = (
        P(("col", "row"), None),
        P(),
        P("row", "col", None, None),
        P("row", "col"),
        P("row", "col"),
        P("row", "col"),
        P(("row", "col"), None),
    )
    out_specs = (P(("row", "col"), None), P(("col", "row"), None), P())
    return jax.shard_map(
        per_device, mesh=mesh, in_specs=in_specs, out_specs=out_specs, check_vma=False
    )
```

time: 1120 us -> 109 us (0.10)
  waiting for transfers between devices: 1010 us -> 0 us
  Pallas kernels: 0 us -> 98.1 us
  blocking collectives: 63.2 us -> 0 us
  other arithmetic: 15.5 us -> 0 us
  between operations: 14.5 us -> 1.3 us
    psum x1 -> x0, waiting for transfers between devices: 466 us -> none  [per_device(): lax.psum(weight_term, ('row', 'col')) * (1.0 / math.sqrt(nodes_total))]
    reduce_scatter x2 -> x0, waiting for transfers between devices: 332 us -> none  [the longest x1 239 us: per_device(): lax.psum_scatter(partial_value.astype(jnp.bfloat16), 'col', scatter_dimen...]
    all_gather x1 -> x0, waiting for transfers between devices: 210 us -> none  [per_device(): gathered_back = lax.all_gather(back_local, 'col', axis=0, tiled=True)]
    pallas_call x0 -> x1, Pallas kernels: none -> 98.1 us  [per_device(): pl.pallas_call(functools.partial(kernel, 1.0 / math.sqrt(nodes)), out_sha...]
    all_gather x1 -> x0, blocking collectives: 63.2 us -> none  [per_device(): source = lax.all_gather(features, 'row', axis=0, tiled=True)]
  transfers between devices with their start and end apart: 4 -> 0, of which waited for: 4 -> 0; matrix products, arithmetic and copies ran while one was open for 2% -> 0% of each run, Pallas kernels for 0% -> 0%
where the time goes in v1:
time: 109 us; the launch traced here: 107 us
  Pallas kernels  98.1 us (90%)
  local copies, waits for them, and re-layouts  7.83 us (7%)
  between operations  1.3 us (1%)
    pallas_call x1, Pallas kernels, per_device(): pl.pallas_call(functools.partial(kernel, 1.0 / math.sqrt(nodes)), out_sha...  98.1 us
    unnamed x15, local copies, waits for them, and re-layouts  7.83 us

profile of v1, /device:TPU:1, one launch (start us, length us, event | category | flops | bytes accessed | tf_op | source)
XLA Modules:
  0.0 107.3 jit_solution(17404198368380194556)
XLA Ops:
  1.3 0.0 copy-start
  1.3 2.2 %copy-done = bf16[1,128,128,128]{3,2,1,0:T(8,128)(2,1)S(1)} copy-done((bf16[1,128,128,128]{3,2,1,0:T(8,128)(2,1)S(1)}, bf16[1,128,128,128]{3,2,1,0:T(8,128)(2,1)}, u32[]{:S(2)}) %copy-start) | copy-done | bytes 4194328
  3.5 0.0 copy-start.1
  3.5 0.8 copy-done.1
  4.3 0.0 copy-start.2
  4.3 0.8 copy-done.2
  5.1 0.0 copy-start.3
  5.2 0.8 copy-done.3
  5.9 0.0 copy-start.4
  5.9 0.7 copy-done.4
  6.6 0.0 copy-start.5
  6.6 0.7 copy-done.5
  7.2 98.1 %shard_map.94 = (bf16[128,256]{1,0:T(8,128)(2,1)S(1)}, bf16[128,128]{1,0:T(8,128)(2,1)S(1)}, f32[128,256]{1,0:T(8,128)S(1)}) custom-call(bf16[128,128]{1,0:T(8,128)(2,1)S(1)} %copy-done.3, bf16[128,256]{1,0:T(8,128)(2,1)S(1)} %copy-done.1, bf16[1,128,128,128]{3,2,1,0:T(8,128)(2,1)S(1)} %copy-done, s32[1,128]{1,0:T(1,128)S(1)} %copy-done.4, ...), custom_call_target="tpu_custom_call" | custom-call | flops 1073741824 | bytes 4194304 | tf_op jit(solution)/shard_map/pallas_call | solution.py:291
  105.4 0.6 copy.14
  106.0 0.6 copy.15
  106.6 0.7 copy.16
Async XLA Ops:
  1.3 2.2 %copy-start = (bf16[1,128,128,128]{3,2,1,0:T(8,128)(2,1)S(1)}, bf16[1,128,128,128]{3,2,1,0:T(8,128)(2,1)}, u32[]{:S(2)}) copy-start(bf16[1,128,128,128]{3,2,1,0:T(8,128)(2,1)} %vals_hbm.1) | copy-start | bytes 12582916
  3.5 0.8 copy-start.1
  4.3 0.8 copy-start.2
  5.1 0.8 copy-start.3
  5.9 0.7 copy-start.4
  6.6 0.7 copy-start.5

commit v2 on v1

v2 whole, which is shorter than its diff:
```python
import functools
import math

import jax
import jax.numpy as jnp
from jax import lax
from jax.experimental import pallas as pl
from jax.experimental.pallas import tpu as pltpu
from jax.sharding import PartitionSpec as P

MESH = pl.DeviceIdType.MESH
F32 = jnp.float32
BF16 = jnp.bfloat16
T = 128

NX, NZ, NY, NH, NC = 4, 8, 4, 2, 2


def order_tables(target, source, live, bins):
    slots = target.shape[1]
    lane = lax.broadcasted_iota(jnp.int32, (slots, slots), 1)
    sub = lax.broadcasted_iota(jnp.int32, (slots, slots), 0)
    wide = jnp.where(lane < live, jnp.broadcast_to(target, (slots, slots)), bins)
    key = wide * slots + lane
    tall = wide.T
    tall_key = tall * slots + sub
    rank = jnp.sum((tall_key < key).astype(jnp.int32), axis=0, keepdims=True)
    tall_rank = jnp.broadcast_to(rank, (slots, slots)).T
    placed = tall_rank == lane
    tall_source = jnp.broadcast_to(source, (slots, slots)).T
    perm = jnp.sum(jnp.where(placed, sub, 0), axis=0, keepdims=True)
    src = jnp.sum(jnp.where(placed, tall_source, 0), axis=0, keepdims=True)
    place = jnp.sum(jnp.where(placed, tall, 0), axis=0, keepdims=True)
    before = jnp.sum(jnp.where(tall_rank + 1 == lane, tall, 0), axis=0, keepdims=True)
    first = lax.broadcasted_iota(jnp.int32, (1, slots), 1) == 0
    keep = jnp.where((place == before) & jnp.logical_not(first), 1, 0)
    upto = jnp.sum((tall <= lane).astype(jnp.int32), axis=0, keepdims=True)
    here = jnp.sum((tall == lane).astype(jnp.int32), axis=0, keepdims=True)
    last = jnp.where(here > 0, upto - 1, slots)
    return perm, src, keep, last


def kernel(
    scale,
    feat_hbm, weight_hbm, vals_hbm, row_hbm, col_hbm, count_hbm, up_hbm,
    act_ref, fg_ref, wg_ref,
    weight_ref, row_ref, col_ref, up_ref, count_ref,
    vals, xbuf, sums, pbuf, rx, zs, rz, bbuf, qpack, rq, ys, ry, zh, rzh,
    wown, wr1, wz, wrz, wall,
    tabv, tabs,
    local_sem, x_send, x_recv, px_send, px_recv, pz_send, pz_recv, b_send, b_recv,
    qc_send, qc_recv, qy_send, qy_recv, qh_send, qh_recv,
    w1_send, w1_recv, wz_send, wz_recv, w2_send, w2_recv,
):
    r = lax.axis_index("row")
    c = lax.axis_index("col")
    y, h, core = r // (NH * NC), (r // NC) % NH, r % NC
    z, x = c // NX, c % NX
    slots = vals.shape[0]
    sent = []

    def rowdev(yy, hh, cc):
        return {"row": (yy * NH + hh) * NC + cc, "col": c}

    def coldev(zz, xx):
        return {"row": r, "col": zz * NX + xx}

    def send(src, dst, send_sem, recv_sem, device):
        copy = pltpu.make_async_remote_copy(
            src_ref=src, dst_ref=dst, send_sem=send_sem, recv_sem=recv_sem, device_id=device, device_id_type=MESH
        )
        copy.start()
        sent.append(copy)

    def arrived(dst, recv_sem):
        pltpu.make_async_remote_copy(
            src_ref=dst, dst_ref=dst, send_sem=recv_sem, recv_sem=recv_sem, device_id=rowdev(y, h, 1 - core), device_id_type=MESH
        ).wait_recv()

    group = NX * NY * NC
    ring = NH * NZ
    place = (x * NY + y) * NC + core
    spot = h * NZ + z

    def group_device(p):
        return {"row": ((p // NC) % NY * NH + h) * NC + p % NC, "col": z * NX + p // (NY * NC)}

    def ring_device(p):
        return {"row": (y * NH + p // NZ) * NC + core, "col": (p % NZ) * NX + x}

    barrier = pltpu.get_barrier_semaphore()

    def greet_ring(g, carry):
        pl.semaphore_signal(barrier, inc=1, device_id=ring_device((spot + g) % ring), device_id_type=MESH)
        return carry

    def greet_group(g, carry):
        pl.semaphore_signal(barrier, inc=1, device_id=group_device((place + g) % group), device_id_type=MESH)
        return carry

    pl.semaphore_signal(barrier, inc=1, device_id=rowdev(y, 1 - h, core), device_id_type=MESH)
    lax.fori_loop(1, ring // 2, greet_ring, 0)
    lax.fori_loop(ring // 2 + 1, ring, greet_ring, 0)
    lax.fori_loop(1, group, greet_group, 0)
    own_copies = [
        pltpu.make_async_copy(src, dst, local_sem.at[i])
        for i, (src, dst) in enumerate([
            (row_hbm, row_ref), (col_hbm, col_ref), (count_hbm, count_ref), (feat_hbm, xbuf.at[r]),
            (weight_hbm, weight_ref), (up_hbm, up_ref), (vals_hbm.at[0], vals),
        ])
    ]
    for copy in own_copies:
        copy.start()
    pl.semaphore_wait(barrier, ring + group - 2)

    def tile_of(yy, hh, cc):
        return (yy * NH + hh) * NC + cc

    n = [0]

    def share(tile, device):
        send(xbuf.at[tile], xbuf.at[tile], x_send.at[n[0]], x_recv.at[tile], device)
        n[0] += 1

    def share_own(device):
        send(feat_hbm, xbuf.at[r], x_send.at[n[0]], x_recv.at[r], device)
        n[0] += 1

    share_own(rowdev(y, 1 - h, core))
    for d in range(1, NY):
        share_own(rowdev((y + d) % NY, h, core))
    share_own(rowdev(y, h, 1 - core))
    for copy in own_copies[:3]:
        copy.wait()
    live = count_ref[0, 0]
    forward = order_tables(row_ref[...], col_ref[...], live, NZ * NX)
    for i, table in enumerate(forward):
        tabv[i : i + 1, :] = table
    backward = order_tables(col_ref[...], row_ref[...], live, NY * NH * NC)
    for i, table in enumerate(backward):
        tabv[4 + i : 5 + i, :] = table
    tabs_copy = pltpu.make_async_copy(tabv, tabs, local_sem.at[7])
    tabs_copy.start()
    sums[slots] = jnp.zeros((T, T), BF16)
    def pass_on(hh):
        for d in (1, 3, 2):
            tile = tile_of((y + d) % NY, hh, core)
            arrived(xbuf.at[tile], x_recv.at[tile])
            share(tile, rowdev(y, h, 1 - core))

    pass_on(h)
    other = tile_of(y, 1 - h, core)
    arrived(xbuf.at[other], x_recv.at[other])
    for d in range(1, NY):
        share(other, rowdev((y + d) % NY, h, core))
    share(other, rowdev(y, h, 1 - core))
    pass_on(1 - h)
    for hh in range(NH):
        for yy in range(NY):
            tile = tile_of(yy, hh, 1 - core)
            arrived(xbuf.at[tile], x_recv.at[tile])

    tabs_copy.wait()
    for copy in own_copies[3:]:
        copy.wait()

    def product_scan(base, multiply):
        def body(step, total):
            for u in range(8):
                k = step * 8 + u
                keep = tabs[base + 2, k].astype(F32)
                total = total * keep + multiply(tabs[base, k], tabs[base + 1, k])
                sums[k] = total.astype(BF16)
            return total

        lax.fori_loop(0, slots // 8, body, jnp.zeros((T, T), F32))

    product_scan(0, lambda i, s: jnp.dot(vals[i], xbuf[s], preferred_element_type=F32))

    def near(k):
        side = jnp.minimum(z, NZ - 1 - z)
        both = k <= 2 * side
        far = jnp.where(both, (k + 1) // 2, k - side)
        up = jnp.where(both, k % 2 == 1, z < NZ // 2)
        return z + jnp.where(up, far, -far)

    order = [near(k) for k in range(NZ - 1, 0, -1)] + [z]
    for zz in order:
        for xx in range(NX):
            pbuf[xx, zz] = sums[tabs[3, zz * NX + xx]]
        for d in range(1, NX):
            send(
                pbuf.at[(x + d) % NX, zz], rx.at[d - 1, zz],
                px_send.at[d - 1, zz], px_recv.at[d - 1, zz], coldev(z, (x + d) % NX),
            )
    for o, zz in enumerate(order):
        total = pbuf[x, zz].astype(F32)
        for d in range(1, NX):
            arrived(rx.at[d - 1, zz], px_recv.at[d - 1, zz])
            total += rx[d - 1, zz].astype(F32)
        if o < NZ - 1:
            zs[zz] = total.astype(BF16)
            send(zs.at[zz], rz.at[z], pz_send.at[zz], pz_recv.at[z], coldev(zz, x))
    for zz in order[:-1]:
        arrived(rz.at[zz], pz_recv.at[zz])
        total += rz[zz].astype(F32)
    aggregated = total.astype(BF16)

    weight = weight_ref[...]
    summed = jnp.dot(aggregated, weight, preferred_element_type=F32)
    sigma = jax.nn.sigmoid(summed)
    slope = sigma * (1.0 + summed * (1.0 - sigma))
    grad_rows = (up_ref[...].astype(F32) * slope).astype(BF16)
    back = lax.dot_general(weight, grad_rows, (((1,), (1,)), ((), ())), preferred_element_type=F32)
    bbuf[c] = back.astype(BF16)

    side = z + 1 - 2 * (z % 2)
    turn = 2 - 4 * (z // 2 % 2)
    mates = [side, z + turn, side + turn]
    across = (z + NZ // 2) % NZ
    for zz in [across] + mates:
        send(bbuf.at[c], bbuf.at[c], b_send.at[0, zz], b_recv.at[c], coldev(zz, x))
    for d in range(1, NX):
        send(bbuf.at[c], bbuf.at[c], b_send.at[d, z], b_recv.at[c], coldev(z, (x + d) % NX))
    act_ref[...] = (summed * sigma).astype(BF16)
    term = jnp.dot(aggregated.astype(F32).T.astype(BF16), grad_rows, preferred_element_type=F32)
    high, wide = wown.shape[1:]
    blocks = [(i * high, j * wide) for i in range(term.shape[0] // high) for j in range(term.shape[1] // wide)]
    for i, (top, left) in enumerate(blocks):
        wown[i] = term[top : top + high, left : left + wide]
    def give_pieces(g, carry):
        p = (place + g) % group
        pltpu.make_async_remote_copy(
            src_ref=wown.at[p], dst_ref=wr1.at[place], send_sem=w1_send.at[p], recv_sem=w1_recv.at[place],
            device_id=group_device(p), device_id_type=MESH,
        ).start()
        return carry

    lax.fori_loop(1, group, give_pieces, 0)
    for i, zz in enumerate([side, across] + mates[1:] + [(mate + NZ // 2) % NZ for mate in mates]):
        t = zz * NX + x
        arrived(bbuf.at[t], b_recv.at[t])
        if i == 1:
            for mate in mates:
                send(bbuf.at[t], bbuf.at[t], b_send.at[0, (mate + NZ // 2) % NZ], b_recv.at[t], coldev(mate, x))
        for d in range(1, NX):
            send(bbuf.at[t], bbuf.at[t], b_send.at[d, zz], b_recv.at[t], coldev(z, (x + d) % NX))

    def take_pieces(g, total):
        p = (place + g) % group
        arrived(wr1.at[p], w1_recv.at[p])
        return total + wr1[p]

    piece = lax.fori_loop(1, group, take_pieces, wown[place])
    wz[...] = piece

    def give_ring(g, carry):
        p = (spot + g) % ring
        pltpu.make_async_remote_copy(
            src_ref=wz, dst_ref=wrz.at[spot], send_sem=wz_send.at[p], recv_sem=wz_recv.at[spot],
            device_id=ring_device(p), device_id_type=MESH,
        ).start()
        return carry

    lax.fori_loop(1, ring, give_ring, 0)
    for k in range(NZ):
        for d in range(1, NX):
            t = (near(k) if k else z) * NX + (x + d) % NX
            arrived(bbuf.at[t], b_recv.at[t])

    product_scan(4, lambda i, s: jnp.dot(bbuf[s], vals[i], preferred_element_type=F32))

    for o in range(1, NY + 1):
        yy = (y + o) % NY
        for cc in range(NC):
            for hh in range(NH):
                qpack[cc, yy, hh] = sums[tabs[7, tile_of(yy, hh, cc)]]
        send(
            qpack.at[1 - core, yy], rq.at[yy], qc_send.at[o - 1], qc_recv.at[yy], rowdev(y, h, 1 - core)
        )
    for o in range(1, NY + 1):
        yy = (y + o) % NY
        arrived(rq.at[yy], qc_recv.at[yy])
        pair = qpack[core, yy].astype(F32) + rq[yy].astype(F32)
        if o < NY:
            ys[o - 1] = pair.astype(BF16)
            send(ys.at[o - 1], ry.at[o - 1], qy_send.at[o - 1], qy_recv.at[o - 1], rowdev(yy, h, core))
        else:
            ys[o - 1] = pair.astype(BF16)
    for o in range(1, NY):
        arrived(ry.at[o - 1], qy_recv.at[o - 1])
    away = ys[NY - 1, 1 - h].astype(F32)
    mine = ys[NY - 1, h].astype(F32)
    for o in range(1, NY):
        away += ry[o - 1, 1 - h].astype(F32)
    zh[...] = away.astype(BF16)
    send(zh, rzh, qh_send, qh_recv, rowdev(y, 1 - h, core))
    for o in range(1, NY):
        mine += ry[o - 1, h].astype(F32)
    def take_ring(g, total):
        p = (spot + g) % ring
        arrived(wrz.at[p], wz_recv.at[p])
        return total + wrz[p]

    wall[place] = lax.fori_loop(1, ring, take_ring, piece) * scale

    def give_sums(g, carry):
        p = (place + g) % group
        pltpu.make_async_remote_copy(
            src_ref=wall.at[place], dst_ref=wall.at[place], send_sem=w2_send.at[p], recv_sem=w2_recv.at[place],
            device_id=group_device(p), device_id_type=MESH,
        ).start()
        return carry

    lax.fori_loop(1, group, give_sums, 0)

    def take_sums(g, carry):
        p = (place + g) % group
        arrived(wall.at[p], w2_recv.at[p])
        return carry

    lax.fori_loop(1, group, take_sums, 0)
    for i, (top, left) in enumerate(blocks):
        wg_ref[top : top + high, left : left + wide] = wall[i]
    arrived(rzh, qh_recv)
    fg_ref[...] = (mine + rzh[...].astype(F32)).T.astype(BF16)
    for copy in sent:
        copy.wait_send()

    def sent_group(g, carry):
        p = (place + g) % group
        for src, sem in ((wown.at[p], w1_send.at[p]), (wall.at[place], w2_send.at[p])):
            pltpu.make_async_remote_copy(
                src_ref=src, dst_ref=src, send_sem=sem, recv_sem=sem,
                device_id=group_device(p), device_id_type=MESH,
            ).wait_send()
        return carry

    def sent_ring(g, carry):
        p = (spot + g) % ring
        pltpu.make_async_remote_copy(
            src_ref=wz, dst_ref=wz, send_sem=wz_send.at[p], recv_sem=wz_send.at[p],
            device_id=ring_device(p), device_id_type=MESH,
        ).wait_send()
        return carry

    lax.fori_loop(1, group, sent_group, 0)
    lax.fori_loop(1, ring, sent_ring, 0)


def per_device(features, weight, tile_values, tile_row, tile_col, tile_count, upstream):
    rows, width = features.shape
    hidden = weight.shape[1]
    slots = tile_values.shape[1]
    nodes = rows * lax.axis_size("row") * lax.axis_size("col")
    tile = (T, T)
    group = NX * NY * NC
    ring = NH * NZ
    piece = (8, 128)
    dma = pltpu.SemaphoreType.DMA
    vm = pl.BlockSpec(memory_space=pltpu.VMEM)
    hbm = pl.BlockSpec(memory_space=pl.ANY)
    flops = 2 * 2 * slots * T * T * T
    return pl.pallas_call(
        functools.partial(kernel, 1.0 / math.sqrt(nodes)),
        out_shape=(
            pltpu.VMEM((rows, hidden), BF16),
            pltpu.VMEM((rows, width), BF16),
            pltpu.VMEM((width, hidden), F32),
        ),
        in_specs=[hbm] * 7,
        out_specs=(vm, vm, vm),
        scratch_shapes=[
            pltpu.VMEM(weight.shape, BF16),
            pltpu.VMEM(tile_row.shape, jnp.int32),
            pltpu.VMEM(tile_col.shape, jnp.int32),
            pltpu.VMEM(upstream.shape, BF16),
            pltpu.SMEM(tile_count.shape, jnp.int32),
            pltpu.VMEM((slots,) + tile, BF16),
            pltpu.VMEM((NY * NH * NC,) + tile, BF16),
            pltpu.VMEM((slots + 1,) + tile, BF16),
            pltpu.VMEM((NX, NZ) + tile, BF16),
            pltpu.VMEM((NX - 1, NZ) + tile, BF16),
            pltpu.VMEM((NZ,) + tile, BF16),
            pltpu.VMEM((NZ,) + tile, BF16),
            pltpu.VMEM((NZ * NX,) + tile, BF16),
            pltpu.VMEM((NC, NY, NH) + tile, BF16),
            pltpu.VMEM((NY, NH) + tile, BF16),
            pltpu.VMEM((NY, NH) + tile, BF16),
            pltpu.VMEM((max(NY - 1, 1), NH) + tile, BF16),
            pltpu.VMEM(tile, BF16),
            pltpu.VMEM(tile, BF16),
            pltpu.VMEM((group,) + piece, F32),
            pltpu.VMEM((group,) + piece, F32),
            pltpu.VMEM(piece, F32),
            pltpu.VMEM((ring,) + piece, F32),
            pltpu.VMEM((group,) + piece, F32),
            pltpu.VMEM((8, slots), jnp.int32),
            pltpu.SMEM((8, slots), jnp.int32),
            dma((8,)),
            dma((NY * NH * NC,)), dma((NY * NH * NC,)),
            dma((NX - 1, NZ)), dma((NX - 1, NZ)),
            dma((NZ,)), dma((NZ,)),
            dma((NX, NZ)), dma((NZ * NX,)),
            dma((NY,)), dma((NY,)),
            dma((max(NY - 1, 1),)), dma((max(NY - 1, 1),)),
            dma, dma,
            dma((group,)), dma((group,)),
            dma((ring,)), dma((ring,)),
            dma((group,)), dma((group,)),
        ],
        compiler_params=pltpu.CompilerParams(
            collective_id=0, has_side_effects=True, vmem_limit_bytes=56 * 1024 * 1024
        ),
        cost_estimate=pl.CostEstimate(flops=flops, bytes_accessed=slots * T * T * 2, transcendentals=rows * hidden),
    )(features, weight, tile_values, tile_row, tile_col, tile_count, upstream)


def solution(mesh):
    in_specs = (
        P(("col", "row"), None),
        P(),
        P("row", "col", None, None),
        P("row", "col"),
        P("row", "col"),
        P("row", "col"),
        P(("row", "col"), None),
    )
    out_specs = (P(("row", "col"), None), P(("col", "row"), None), P())
    return jax.shard_map(
        per_device, mesh=mesh, in_specs=in_specs, out_specs=out_specs, check_vma=False
    )
```

time: 109 us -> 93.8 us (0.86); the launches traced: 107 us -> 93.7 us
  Pallas kernels: 98.1 us -> 90.5 us
  local copies, waits for them, and re-layouts: 7.83 us -> 1.9 us
    pallas_call x1, Pallas kernels: 98.1 us -> 90.5 us  [per_device(): pl.pallas_call(functools.partial(kernel, 1.0 / math.sqrt(nodes)), out_sha...]
    unnamed x15 -> x3, local copies, waits for them, and re-layouts: 7.83 us -> 1.9 us
where the time goes in v2:
time: 93.8 us; the launch traced here: 93.7 us
  Pallas kernels  90.5 us (96%)
  local copies, waits for them, and re-layouts  1.9 us (2%)
  between operations  1.29 us (1%)
    pallas_call x1, Pallas kernels, per_device(): pl.pallas_call(functools.partial(kernel, 1.0 / math.sqrt(nodes)), out_sha...  90.5 us
    unnamed x3, local copies, waits for them, and re-layouts  1.9 us

profile of v2, /device:TPU:1, one launch (start us, length us, event | category | flops | bytes accessed | tf_op | source)
XLA Modules:
  0.0 93.7 jit_solution(12192515324277245494)
XLA Ops:
  1.3 90.5 %shard_map.94 = (bf16[128,256]{1,0:T(8,128)(2,1)S(1)}, bf16[128,128]{1,0:T(8,128)(2,1)S(1)}, f32[128,256]{1,0:T(8,128)S(1)}) custom-call(bf16[128,128]{1,0:T(8,128)(2,1)} %feat_hbm.1, bf16[128,256]{1,0:T(8,128)(2,1)} %weight_hbm.1, bf16[1,128,128,128]{3,2,1,0:T(8,128)(2,1)} %vals_hbm.1, s32[1,128]{1,0:T(1,128)} %row_hbm.1, s32[1,128]{1,0:T(1,128)} %col_hbm.1, ...), custom_call_target="tpu_custom_call" | custom-call | flops 1073741824 | bytes 4194304 | tf_op jit(solution)/shard_map/pallas_call | solution.py:364
  91.8 0.6 copy.13
  92.4 0.6 copy.14
  93.0 0.7 copy.15

commit v3 on v2

v3 whole, which is shorter than its diff:
```python
import functools
import math

import jax
import jax.numpy as jnp
from jax import lax
from jax.experimental import pallas as pl
from jax.experimental.pallas import tpu as pltpu
from jax.sharding import PartitionSpec as P

MESH = pl.DeviceIdType.MESH
F32 = jnp.float32
BF16 = jnp.bfloat16
T = 128

NX, NZ, NY, NH, NC = 4, 8, 4, 2, 2
UNROLL = 64


def order_tables(target, source, live, bins):
    slots = target.shape[1]
    lane = lax.broadcasted_iota(jnp.int32, (slots, slots), 1)
    sub = lax.broadcasted_iota(jnp.int32, (slots, slots), 0)
    wide = jnp.where(lane < live, jnp.broadcast_to(target, (slots, slots)), bins)
    key = wide * slots + lane
    tall = wide.T
    tall_key = tall * slots + sub
    rank = jnp.sum((tall_key < key).astype(jnp.int32), axis=0, keepdims=True)
    tall_rank = jnp.broadcast_to(rank, (slots, slots)).T
    placed = tall_rank == lane
    tall_source = jnp.broadcast_to(source, (slots, slots)).T
    perm = jnp.sum(jnp.where(placed, sub, 0), axis=0, keepdims=True)
    src = jnp.sum(jnp.where(placed, tall_source, 0), axis=0, keepdims=True)
    place = jnp.sum(jnp.where(placed, tall, 0), axis=0, keepdims=True)
    before = jnp.sum(jnp.where(tall_rank + 1 == lane, tall, 0), axis=0, keepdims=True)
    first = lax.broadcasted_iota(jnp.int32, (1, slots), 1) == 0
    keep = jnp.where((place == before) & jnp.logical_not(first), 1, 0)
    upto = jnp.sum((tall <= lane).astype(jnp.int32), axis=0, keepdims=True)
    here = jnp.sum((tall == lane).astype(jnp.int32), axis=0, keepdims=True)
    last = jnp.where(here > 0, upto - 1, slots)
    return perm, src, keep, last


def kernel(
    scale,
    feat_hbm, weight_hbm, vals_hbm, row_hbm, col_hbm, count_hbm, up_hbm,
    act_ref, fg_ref, wg_ref,
    weight_ref, row_ref, col_ref, up_ref, count_ref,
    vals, xbuf, sums, pbuf, rx, zs, rz, bbuf, qpack, rq, ys, ry, zh, rzh,
    wown, wr1, wz, wrz, wall,
    tabv, tabs,
    local_sem, x_send, xh_recv, xy_recv, xk_recv, px_send, px_recv, pz_send, pz_recv,
    b_send, bz_recv, bx_recv, q_send, qk_recv, qy_recv, qh_recv,
    w_send, w_recv,
):
    r = lax.axis_index("row")
    c = lax.axis_index("col")
    core, h, y = lax.rem(r, NC), lax.rem(lax.div(r, NC), NH), lax.div(r, NC * NH)
    x, z = lax.rem(c, NX), lax.div(c, NX)
    slots = vals.shape[0]
    on_x = [lax.rem(x + d, NX) for d in range(NX)]
    on_y = [lax.rem(y + d, NY) for d in range(NY)]
    on_h = [h, 1 - h]
    on_core = [core, 1 - core]

    def tile_of(yy, hh, cc):
        return (yy * NH + hh) * NC + cc

    def rowdev(yy, hh, cc):
        return {"row": tile_of(yy, hh, cc), "col": c}

    def coldev(zz, xx):
        return {"row": r, "col": zz * NX + xx}

    group = [(dx, dy, dc) for dx in range(NX) for dy in range(NY) for dc in range(NC)]
    ring = NH * NZ
    spot = h * NZ + z

    def piece_of(xx, yy, cc):
        return (xx * NY + yy) * NC + cc

    def group_device(dx, dy, dc):
        return {"row": tile_of(on_y[dy], h, on_core[dc]), "col": z * NX + on_x[dx]}

    def ring_device(g):
        p = lax.rem(spot + g, ring)
        hh = lax.div(p, NZ)
        return {"row": tile_of(y, hh, core), "col": (p - hh * NZ) * NX + x}

    def send(src, dst, send_sem, recv_sem, device):
        pltpu.make_async_remote_copy(
            src_ref=src, dst_ref=dst, send_sem=send_sem, recv_sem=recv_sem, device_id=device, device_id_type=MESH
        ).start()

    def waiter(ref, sem):
        return pltpu.make_async_remote_copy(
            src_ref=ref, dst_ref=ref, send_sem=sem, recv_sem=sem,
            device_id=rowdev(y, h, on_core[1]), device_id_type=MESH,
        )

    def arrived(ref, sem):
        waiter(ref, sem).wait_recv()

    barrier = pltpu.get_barrier_semaphore()
    peers = [ring_device(g) for g in [ring // 2] + [g for g in range(1, ring) if g != ring // 2]]
    peers += [group_device(*g) for g in group[1:]]
    for peer in peers:
        pl.semaphore_signal(barrier, inc=1, device_id=peer, device_id_type=MESH)
    own_copies = [
        pltpu.make_async_copy(src, dst, local_sem.at[i])
        for i, (src, dst) in enumerate([
            (row_hbm, row_ref), (col_hbm, col_ref), (count_hbm, count_ref), (feat_hbm, xbuf.at[r]),
            (weight_hbm, weight_ref), (up_hbm, up_ref), (vals_hbm.at[0], vals),
        ])
    ]
    for copy in own_copies:
        copy.start()
    pl.semaphore_wait(barrier, len(peers))

    def share(tile, recv_sem, device, src=None):
        send(xbuf.at[tile] if src is None else src, xbuf.at[tile], x_send, recv_sem, device)

    share(r, xh_recv, rowdev(y, on_h[1], core), feat_hbm)
    for d in range(1, NY):
        share(r, xy_recv.at[0, d - 1], rowdev(on_y[d], h, core), feat_hbm)
    share(r, xk_recv, rowdev(y, h, on_core[1]), feat_hbm)
    for copy in own_copies[:3]:
        copy.wait()
    live = count_ref[0, 0]
    forward = order_tables(row_ref[...], col_ref[...], live, NZ * NX)
    for i, table in enumerate(forward):
        tabv[i : i + 1, :] = table
    backward = order_tables(col_ref[...], row_ref[...], live, NY * NH * NC)
    for i, table in enumerate(backward):
        tabv[4 + i : 5 + i, :] = table
    tabs_copy = pltpu.make_async_copy(tabv, tabs, local_sem.at[7])
    tabs_copy.start()
    sums[slots] = jnp.zeros((T, T), BF16)

    for i in range(NH):
        if i == 1:
            other = tile_of(y, on_h[1], core)
            arrived(xbuf.at[other], xh_recv)
            for d in range(1, NY):
                share(other, xy_recv.at[1, d - 1], rowdev(on_y[d], h, core))
            share(other, xk_recv, rowdev(y, h, on_core[1]))
        for d in (1, 3, 2):
            tile = tile_of(on_y[d], on_h[i], core)
            arrived(xbuf.at[tile], xy_recv.at[i, NY - d - 1])
            share(tile, xk_recv, rowdev(y, h, on_core[1]))
    arrived(xbuf.at[pl.ds(0, NY * NH)], xk_recv)

    tabs_copy.wait()
    for copy in own_copies[3:]:
        copy.wait()

    def product_scan(base, multiply):
        def body(step, total):
            for u in range(UNROLL):
                k = step * UNROLL + u
                keep = tabs[base + 2, k].astype(F32)
                total = total * keep + multiply(tabs[base, k], tabs[base + 1, k])
                sums[k] = total.astype(BF16)
            return total

        lax.fori_loop(0, slots // UNROLL, body, jnp.zeros((T, T), F32))

    product_scan(0, lambda i, s: jnp.dot(vals[i], xbuf[s], preferred_element_type=F32))

    def near(k):
        side = jnp.minimum(z, NZ - 1 - z)
        both = k <= 2 * side
        far = jnp.where(both, (k + 1) // 2, k - side)
        up = jnp.where(both, k % 2 == 1, z < NZ // 2)
        return z + jnp.where(up, far, -far)

    order = [near(k) for k in range(NZ - 1, 0, -1)] + [z]
    for zz in order:
        for xx in range(NX):
            pbuf[xx, zz] = sums[tabs[3, zz * NX + xx]]
        for d in (1, 3, 2):
            send(pbuf.at[on_x[d], zz], rx.at[zz, d - 1], px_send, px_recv.at[zz], coldev(z, on_x[d]))
    for o, zz in enumerate(order):
        arrived(rx.at[zz], px_recv.at[zz])
        total = pbuf[x, zz].astype(F32)
        for d in range(1, NX):
            total += rx[zz, d - 1].astype(F32)
        if o < NZ - 1:
            zs[zz] = total.astype(BF16)
            slot = lax.rem(zz - z + NZ, NZ) - 1
            send(zs.at[zz], rz.at[slot], pz_send, pz_recv, coldev(zz, x))
    arrived(rz, pz_recv)
    for o in range(NZ - 1):
        total += rz[o].astype(F32)
    aggregated = total.astype(BF16)

    weight = weight_ref[...]
    summed = jnp.dot(aggregated, weight, preferred_element_type=F32)
    sigma = jax.nn.sigmoid(summed)
    slope = sigma * (1.0 + summed * (1.0 - sigma))
    grad_rows = (up_ref[...].astype(F32) * slope).astype(BF16)
    back = lax.dot_general(weight, grad_rows, (((1,), (1,)), ((), ())), preferred_element_type=F32)
    bbuf[c] = back.astype(BF16)

    side = z + 1 - 2 * lax.rem(z, 2)
    turn = 2 - 4 * lax.rem(lax.div(z, 2), 2)
    mates = [side, z + turn, side + turn]
    across = lax.rem(z + NZ // 2, NZ)
    far = [lax.rem(mate + NZ // 2, NZ) for mate in mates]

    def give_back(t, recv_sem, device):
        send(bbuf.at[t], bbuf.at[t], b_send, recv_sem, device)

    give_back(c, bz_recv.at[0], coldev(across, x))
    for i, mate in enumerate(mates):
        give_back(c, bz_recv.at[1 + i], coldev(mate, x))
    for d in (1, 3, 2):
        give_back(c, bx_recv, coldev(z, on_x[d]))
    act_ref[...] = (summed * sigma).astype(BF16)
    term = jnp.dot(aggregated.astype(F32).T.astype(BF16), grad_rows, preferred_element_type=F32)
    high, wide = wown.shape[1:]
    blocks = [(i * high, j * wide) for i in range(term.shape[0] // high) for j in range(term.shape[1] // wide)]
    for i, (top, left) in enumerate(blocks):
        wown[i] = term[top : top + high, left : left + wide]
    for g, (dx, dy, dc) in enumerate(group[1:]):
        send(
            wown.at[piece_of(on_x[dx], on_y[dy], on_core[dc])], wr1.at[g], w_send.at[0], w_recv.at[0],
            group_device(dx, dy, dc),
        )
    for zz, sem in [(side, 1), (across, 0), (mates[1], 2), (mates[2], 3), (far[0], 4), (far[1], 5), (far[2], 6)]:
        t = zz * NX + x
        arrived(bbuf.at[t], bz_recv.at[sem])
        if sem == 0:
            for i, mate in enumerate(mates):
                give_back(t, bz_recv.at[4 + i], coldev(mate, x))
        for d in (1, 3, 2):
            give_back(t, bx_recv, coldev(z, on_x[d]))

    place = piece_of(x, y, core)
    arrived(wr1, w_recv.at[0])
    piece = wown[place]
    for g in range(len(group) - 1):
        piece += wr1[g]
    wz[...] = piece
    for g in [ring // 2] + [g for g in range(1, ring) if g != ring // 2]:
        send(wz, wrz.at[g - 1], w_send.at[1], w_recv.at[1], ring_device(g))
    arrived(bbuf.at[pl.ds(0, (NX - 1) * NZ)], bx_recv)

    product_scan(4, lambda i, s: jnp.dot(bbuf[s], vals[i], preferred_element_type=F32))

    for j in (1, 0):
        for i in (1, 0):
            for yy in range(NY):
                qpack[j, i, yy] = sums[tabs[7, tile_of(yy, on_h[i], on_core[j])]]
            if j == 1:
                send(qpack.at[j, i], rq.at[i], q_send, qk_recv.at[i], rowdev(y, h, on_core[1]))
    own = {}
    for i in (1, 0):
        arrived(rq.at[i], qk_recv.at[i])
        for d in range(1, NY):
            yy = on_y[d]
            ys[i, d - 1] = (qpack[0, i, yy].astype(F32) + rq[i, yy].astype(F32)).astype(BF16)
            send(ys.at[i, d - 1], ry.at[i, d - 1], q_send, qy_recv.at[i], rowdev(yy, h, core))
        own[i] = qpack[0, i, y].astype(F32) + rq[i, y].astype(F32)
    arrived(ry.at[1], qy_recv.at[1])
    for d in range(NY - 1):
        own[1] += ry[1, d].astype(F32)
    zh[...] = own[1].astype(BF16)
    send(zh, rzh, q_send, qh_recv, rowdev(y, on_h[1], core))
    arrived(wrz, w_recv.at[1])
    for g in range(ring - 1):
        piece += wrz[g]
    wall[place] = piece * scale
    for g in group[1:]:
        send(wall.at[place], wall.at[place], w_send.at[2], w_recv.at[2], group_device(*g))
    arrived(ry.at[0], qy_recv.at[0])
    for d in range(NY - 1):
        own[0] += ry[0, d].astype(F32)
    waiter(xbuf.at[pl.ds(0, NY * NH * NC - 1)], x_send).wait_send()
    waiter(rx, px_send).wait_send()
    waiter(rz, pz_send).wait_send()
    waiter(bbuf.at[pl.ds(0, NZ * NX - 1)], b_send).wait_send()
    waiter(xbuf.at[pl.ds(0, NH * NY + NH * (NY - 1) + 1)], q_send).wait_send()
    waiter(wr1, w_send.at[0]).wait_send()
    waiter(wrz, w_send.at[1]).wait_send()
    waiter(wr1, w_send.at[2]).wait_send()
    arrived(wr1, w_recv.at[2])
    for i, (top, left) in enumerate(blocks):
        wg_ref[top : top + high, left : left + wide] = wall[i]
    arrived(rzh, qh_recv)
    fg_ref[...] = (own[0] + rzh[...].astype(F32)).T.astype(BF16)


def per_device(features, weight, tile_values, tile_row, tile_col, tile_count, upstream):
    rows, width = features.shape
    hidden = weight.shape[1]
    slots = tile_values.shape[1]
    nodes = rows * lax.axis_size("row") * lax.axis_size("col")
    tile = (T, T)
    group = NX * NY * NC
    ring = NH * NZ
    piece = (8, 128)
    dma = pltpu.SemaphoreType.DMA
    vm = pl.BlockSpec(memory_space=pltpu.VMEM)
    hbm = pl.BlockSpec(memory_space=pl.ANY)
    flops = 2 * 2 * slots * T * T * T
    return pl.pallas_call(
        functools.partial(kernel, 1.0 / math.sqrt(nodes)),
        out_shape=(
            pltpu.VMEM((rows, hidden), BF16),
            pltpu.VMEM((rows, width), BF16),
            pltpu.VMEM((width, hidden), F32),
        ),
        in_specs=[hbm] * 7,
        out_specs=(vm, vm, vm),
        scratch_shapes=[
            pltpu.VMEM(weight.shape, BF16),
            pltpu.VMEM(tile_row.shape, jnp.int32),
            pltpu.VMEM(tile_col.shape, jnp.int32),
            pltpu.VMEM(upstream.shape, BF16),
            pltpu.SMEM(tile_count.shape, jnp.int32),
            pltpu.VMEM((slots,) + tile, BF16),
            pltpu.VMEM((NY * NH * NC,) + tile, BF16),
            pltpu.VMEM((slots + 1,) + tile, BF16),
            pltpu.VMEM((NX, NZ) + tile, BF16),
            pltpu.VMEM((NZ, NX - 1) + tile, BF16),
            pltpu.VMEM((NZ,) + tile, BF16),
            pltpu.VMEM((NZ - 1,) + tile, BF16),
            pltpu.VMEM((NZ * NX,) + tile, BF16),
            pltpu.VMEM((NC, NH, NY) + tile, BF16),
            pltpu.VMEM((NH, NY) + tile, BF16),
            pltpu.VMEM((NH, NY - 1) + tile, BF16),
            pltpu.VMEM((NH, NY - 1) + tile, BF16),
            pltpu.VMEM(tile, BF16),
            pltpu.VMEM(tile, BF16),
            pltpu.VMEM((group,) + piece, F32),
            pltpu.VMEM((group - 1,) + piece, F32),
            pltpu.VMEM(piece, F32),
            pltpu.VMEM((ring - 1,) + piece, F32),
            pltpu.VMEM((group,) + piece, F32),
            pltpu.VMEM((8, slots), jnp.int32),
            pltpu.SMEM((8, slots), jnp.int32),
            dma((8,)),
            dma, dma, dma((NH, NY - 1)), dma,
            dma, dma((NZ,)), dma, dma,
            dma, dma((NZ - 1,)), dma,
            dma, dma((NH,)), dma((NH,)), dma,
            dma((3,)), dma((3,)),
        ],
        compiler_params=pltpu.CompilerParams(
            collective_id=0, has_side_effects=True, vmem_limit_bytes=56 * 1024 * 1024
        ),
        cost_estimate=pl.CostEstimate(flops=flops, bytes_accessed=slots * T * T * 2, transcendentals=rows * hidden),
    )(features, weight, tile_values, tile_row, tile_col, tile_count, upstream)


def solution(mesh):
    in_specs = (
        P(("col", "row"), None),
        P(),
        P("row", "col", None, None),
        P("row", "col"),
        P("row", "col"),
        P("row", "col"),
        P(("row", "col"), None),
    )
    out_specs = (P(("row", "col"), None), P(("col", "row"), None), P())
    return jax.shard_map(
        per_device, mesh=mesh, in_specs=in_specs, out_specs=out_specs, check_vma=False
    )
```

time: 93.8 us -> 84.6 us (0.902)
  Pallas kernels: 90.5 us -> 81.2 us
    pallas_call x1, Pallas kernels: 90.5 us -> 81.2 us  [per_device(): pl.pallas_call(functools.partial(kernel, 1.0 / math.sqrt(nodes)), out_sha...]
where the time goes in v3:
time: 84.6 us; the launch traced here: 84.4 us
  Pallas kernels  81.2 us (96%)
  local copies, waits for them, and re-layouts  1.9 us (2%)
  between operations  1.29 us (2%)
    pallas_call x1, Pallas kernels, per_device(): pl.pallas_call(functools.partial(kernel, 1.0 / math.sqrt(nodes)), out_sha...  81.2 us
    unnamed x3, local copies, waits for them, and re-layouts  1.9 us

profile of v3, /device:TPU:1, one launch (start us, length us, event | category | flops | bytes accessed | tf_op | source)
XLA Modules:
  0.0 84.4 jit_solution(12073406771213908950)
XLA Ops:
  1.3 81.2 %shard_map.94 = (bf16[128,256]{1,0:T(8,128)(2,1)S(1)}, bf16[128,128]{1,0:T(8,128)(2,1)S(1)}, f32[128,256]{1,0:T(8,128)S(1)}) custom-call(bf16[128,128]{1,0:T(8,128)(2,1)} %feat_hbm.1, bf16[128,256]{1,0:T(8,128)(2,1)} %weight_hbm.1, bf16[1,128,128,128]{3,2,1,0:T(8,128)(2,1)} %vals_hbm.1, s32[1,128]{1,0:T(1,128)} %row_hbm.1, s32[1,128]{1,0:T(1,128)} %col_hbm.1, ...), custom_call_target="tpu_custom_call" | custom-call | flops 1073741824 | bytes 4194304 | tf_op jit(solution)/shard_map/pallas_call | solution.py:307
  82.5 0.6 copy.13
  83.2 0.6 copy.14
  83.8 0.7 copy.15

commit v4 on v3

--- a/solution.py
+++ b/solution.py
@@ -115,15 +115,16 @@
     ]
     for copy in own_copies:
         copy.start()
+    own_copies[3].wait()
     pl.semaphore_wait(barrier, len(peers))
 
-    def share(tile, recv_sem, device, src=None):
-        send(xbuf.at[tile] if src is None else src, xbuf.at[tile], x_send, recv_sem, device)
-
-    share(r, xh_recv, rowdev(y, on_h[1], core), feat_hbm)
+    def share(tile, recv_sem, device):
+        send(xbuf.at[tile], xbuf.at[tile], x_send, recv_sem, device)
+
+    share(r, xh_recv, rowdev(y, on_h[1], core))
     for d in range(1, NY):
-        share(r, xy_recv.at[0, d - 1], rowdev(on_y[d], h, core), feat_hbm)
-    share(r, xk_recv, rowdev(y, h, on_core[1]), feat_hbm)
+        share(r, xy_recv.at[0, d - 1], rowdev(on_y[d], h, core))
+    share(r, xk_recv, rowdev(y, h, on_core[1]))
     for copy in own_copies[:3]:
         copy.wait()
     live = count_ref[0, 0]
@@ -151,7 +152,7 @@
     arrived(xbuf.at[pl.ds(0, NY * NH)], xk_recv)
 
     tabs_copy.wait()
-    for copy in own_copies[3:]:
+    for copy in own_copies[4:]:
         copy.wait()
 
     def product_scan(base, multiply):
@@ -227,14 +228,16 @@
             wown.at[piece_of(on_x[dx], on_y[dy], on_core[dc])], wr1.at[g], w_send.at[0], w_recv.at[0],
             group_device(dx, dy, dc),
         )
-    for zz, sem in [(side, 1), (across, 0), (mates[1], 2), (mates[2], 3), (far[0], 4), (far[1], 5), (far[2], 6)]:
-        t = zz * NX + x
+    last = NZ - 1
+    for zz, sem in [(side, 1), (across, 0), (mates[1], 2), (mates[2], 3), (across, last), (far[0], 4), (far[1], 5), (far[2], 6)]:
+        t = zz * NX + (on_x[2] if sem == last else x)
         arrived(bbuf.at[t], bz_recv.at[sem])
-        if sem == 0:
+        if sem in (0, last):
             for i, mate in enumerate(mates):
-                give_back(t, bz_recv.at[4 + i], coldev(mate, x))
-        for d in (1, 3, 2):
-            give_back(t, bx_recv, coldev(z, on_x[d]))
+                give_back(t, bx_recv if sem == last else bz_recv.at[4 + i], coldev(mate, x))
+        if sem != last:
+            for d in (1, 3, 2)[: 2 if sem >= 4 else 3]:
+                give_back(t, bz_recv.at[last] if (sem, d) == (0, 2) else bx_recv, coldev(z, on_x[d]))
 
     place = piece_of(x, y, core)
     arrived(wr1, w_recv.at[0])
@@ -244,7 +247,7 @@
     wz[...] = piece
     for g in [ring // 2] + [g for g in range(1, ring) if g != ring // 2]:
         send(wz, wrz.at[g - 1], w_send.at[1], w_recv.at[1], ring_device(g))
-    arrived(bbuf.at[pl.ds(0, (NX - 1) * NZ)], bx_recv)
+    arrived(bbuf.at[pl.ds(0, (NX - 1) * NZ - 1)], bx_recv)
 
     product_scan(4, lambda i, s: jnp.dot(bbuf[s], vals[i], preferred_element_type=F32))
 
@@ -343,7 +346,7 @@
             dma((8,)),
             dma, dma, dma((NH, NY - 1)), dma,
             dma, dma((NZ,)), dma, dma,
-            dma, dma((NZ - 1,)), dma,
+            dma, dma((NZ,)), dma,
             dma, dma((NH,)), dma((NH,)), dma,
             dma((3,)), dma((3,)),
         ],

time: 84.6 us -> 83.2 us (0.983); the launches traced: 84.4 us -> 82.1 us
  Pallas kernels: 81.2 us -> 78.9 us
    pallas_call x1, Pallas kernels: 81.2 us -> 78.9 us  [per_device(): pl.pallas_call(functools.partial(kernel, 1.0 / math.sqrt(nodes)), out_sha...]
where the time goes in v4:
time: 83.2 us; the launch traced here: 82.1 us
  Pallas kernels  78.9 us (95%)
  local copies, waits for them, and re-layouts  1.9 us (2%)
  between operations  1.29 us (2%)
    pallas_call x1, Pallas kernels, per_device(): pl.pallas_call(functools.partial(kernel, 1.0 / math.sqrt(nodes)), out_sha...  78.9 us
    unnamed x3, local copies, waits for them, and re-layouts  1.9 us

profile of v4, /device:TPU:1, one launch (start us, length us, event | category | flops | bytes accessed | tf_op | source)
XLA Modules:
  0.0 82.1 jit_solution(10619399195774714553)
XLA Ops:
  1.3 78.9 %shard_map.94 = (bf16[128,256]{1,0:T(8,128)(2,1)S(1)}, bf16[128,128]{1,0:T(8,128)(2,1)S(1)}, f32[128,256]{1,0:T(8,128)S(1)}) custom-call(bf16[128,128]{1,0:T(8,128)(2,1)} %feat_hbm.1, bf16[128,256]{1,0:T(8,128)(2,1)} %weight_hbm.1, bf16[1,128,128,128]{3,2,1,0:T(8,128)(2,1)} %vals_hbm.1, s32[1,128]{1,0:T(1,128)} %row_hbm.1, s32[1,128]{1,0:T(1,128)} %col_hbm.1, ...), custom_call_target="tpu_custom_call" | custom-call | flops 1073741824 | bytes 4194304 | tf_op jit(solution)/shard_map/pallas_call | solution.py:310
  80.2 0.6 copy.13
  80.8 0.6 copy.14
  81.4 0.7 copy.15

commit v5 on v4

--- a/solution.py
+++ b/solution.py
@@ -233,7 +233,7 @@
         t = zz * NX + (on_x[2] if sem == last else x)
         arrived(bbuf.at[t], bz_recv.at[sem])
         if sem in (0, last):
-            for i, mate in enumerate(mates):
+            for i, mate in reversed(list(enumerate(mates))):
                 give_back(t, bx_recv if sem == last else bz_recv.at[4 + i], coldev(mate, x))
         if sem != last:
             for d in (1, 3, 2)[: 2 if sem >= 4 else 3]:

time: 83.2 us -> 82.3 us (0.989)
  no operation moved by 1% of the time
where the time goes in v5:
time: 82.3 us; the launch traced here: 81.7 us
  Pallas kernels  78.5 us (95%)
  local copies, waits for them, and re-layouts  1.9 us (2%)
  between operations  1.29 us (2%)
    pallas_call x1, Pallas kernels, per_device(): pl.pallas_call(functools.partial(kernel, 1.0 / math.sqrt(nodes)), out_sha...  78.5 us
    unnamed x3, local copies, waits for them, and re-layouts  1.9 us

profile of v5, /device:TPU:1, one launch (start us, length us, event | category | flops | bytes accessed | tf_op | source)
XLA Modules:
  0.0 81.7 jit_solution(17529649937438988987)
XLA Ops:
  1.3 78.5 %shard_map.94 = (bf16[128,256]{1,0:T(8,128)(2,1)S(1)}, bf16[128,128]{1,0:T(8,128)(2,1)S(1)}, f32[128,256]{1,0:T(8,128)S(1)}) custom-call(bf16[128,128]{1,0:T(8,128)(2,1)} %feat_hbm.1, bf16[128,256]{1,0:T(8,128)(2,1)} %weight_hbm.1, bf16[1,128,128,128]{3,2,1,0:T(8,128)(2,1)} %vals_hbm.1, s32[1,128]{1,0:T(1,128)} %row_hbm.1, s32[1,128]{1,0:T(1,128)} %col_hbm.1, ...), custom_call_target="tpu_custom_call" | custom-call | flops 1073741824 | bytes 4194304 | tf_op jit(solution)/shard_map/pallas_call | solution.py:310
  79.8 0.6 copy.13
  80.5 0.6 copy.14
  81.1 0.7 copy.15

commit v6 on v5

--- a/solution.py
+++ b/solution.py
@@ -14,7 +14,7 @@
 T = 128
 
 NX, NZ, NY, NH, NC = 4, 8, 4, 2, 2
-UNROLL = 64
+UNROLL = 128
 
 
 def order_tables(target, source, live, bins):

time: 82.3 us -> 81.9 us (level)
  no operation moved by 1% of the time
where the time goes in v6:
time: 81.9 us; the launch traced here: 81.5 us
  Pallas kernels  78.3 us (96%)
  local copies, waits for them, and re-layouts  1.9 us (2%)
  between operations  1.29 us (2%)
    pallas_call x1, Pallas kernels, per_device(): pl.pallas_call(functools.partial(kernel, 1.0 / math.sqrt(nodes)), out_sha...  78.3 us
    unnamed x3, local copies, waits for them, and re-layouts  1.9 us

profile of v6, /device:TPU:1, one launch (start us, length us, event | category | flops | bytes accessed | tf_op | source)
XLA Modules:
  0.0 81.5 jit_solution(31652217010523663)
XLA Ops:
  1.3 78.3 %shard_map.94 = (bf16[128,256]{1,0:T(8,128)(2,1)S(1)}, bf16[128,128]{1,0:T(8,128)(2,1)S(1)}, f32[128,256]{1,0:T(8,128)S(1)}) custom-call(bf16[128,128]{1,0:T(8,128)(2,1)} %feat_hbm.1, bf16[128,256]{1,0:T(8,128)(2,1)} %weight_hbm.1, bf16[1,128,128,128]{3,2,1,0:T(8,128)(2,1)} %vals_hbm.1, s32[1,128]{1,0:T(1,128)} %row_hbm.1, s32[1,128]{1,0:T(1,128)} %col_hbm.1, ...), custom_call_target="tpu_custom_call" | custom-call | flops 1073741824 | bytes 4194304 | tf_op jit(solution)/shard_map/pallas_call | solution.py:310
  79.6 0.6 copy.13
  80.2 0.6 copy.14
  80.8 0.7 copy.15

commit v7 on v6

--- a/solution.py
+++ b/solution.py
@@ -177,13 +177,12 @@
 
     order = [near(k) for k in range(NZ - 1, 0, -1)] + [z]
     for zz in order:
-        for xx in range(NX):
-            pbuf[xx, zz] = sums[tabs[3, zz * NX + xx]]
         for d in (1, 3, 2):
+            pbuf[on_x[d], zz] = sums[tabs[3, zz * NX + on_x[d]]]
             send(pbuf.at[on_x[d], zz], rx.at[zz, d - 1], px_send, px_recv.at[zz], coldev(z, on_x[d]))
     for o, zz in enumerate(order):
         arrived(rx.at[zz], px_recv.at[zz])
-        total = pbuf[x, zz].astype(F32)
+        total = sums[tabs[3, zz * NX + x]].astype(F32)
         for d in range(1, NX):
             total += rx[zz, d - 1].astype(F32)
         if o < NZ - 1:
@@ -251,20 +250,21 @@
 
     product_scan(4, lambda i, s: jnp.dot(bbuf[s], vals[i], preferred_element_type=F32))
 
-    for j in (1, 0):
-        for i in (1, 0):
-            for yy in range(NY):
-                qpack[j, i, yy] = sums[tabs[7, tile_of(yy, on_h[i], on_core[j])]]
-            if j == 1:
-                send(qpack.at[j, i], rq.at[i], q_send, qk_recv.at[i], rowdev(y, h, on_core[1]))
+    for i in (1, 0):
+        for yy in range(NY):
+            qpack[i, yy] = sums[tabs[7, tile_of(yy, on_h[i], on_core[1])]]
+        send(qpack.at[i], rq.at[i], q_send, qk_recv.at[i], rowdev(y, h, on_core[1]))
+    def mine(i, yy):
+        return sums[tabs[7, tile_of(yy, on_h[i], core)]].astype(F32)
+
     own = {}
     for i in (1, 0):
         arrived(rq.at[i], qk_recv.at[i])
         for d in range(1, NY):
             yy = on_y[d]
-            ys[i, d - 1] = (qpack[0, i, yy].astype(F32) + rq[i, yy].astype(F32)).astype(BF16)
+            ys[i, d - 1] = (mine(i, yy) + rq[i, yy].astype(F32)).astype(BF16)
             send(ys.at[i, d - 1], ry.at[i, d - 1], q_send, qy_recv.at[i], rowdev(yy, h, core))
-        own[i] = qpack[0, i, y].astype(F32) + rq[i, y].astype(F32)
+        own[i] = mine(i, y) + rq[i, y].astype(F32)
     arrived(ry.at[1], qy_recv.at[1])
     for d in range(NY - 1):
         own[1] += ry[1, d].astype(F32)
@@ -330,7 +330,7 @@
             pltpu.VMEM((NZ,) + tile, BF16),
             pltpu.VMEM((NZ - 1,) + tile, BF16),
             pltpu.VMEM((NZ * NX,) + tile, BF16),
-            pltpu.VMEM((NC, NH, NY) + tile, BF16),
+            pltpu.VMEM((NH, NY) + tile, BF16),
             pltpu.VMEM((NH, NY) + tile, BF16),
             pltpu.VMEM((NH, NY - 1) + tile, BF16),
             pltpu.VMEM((NH, NY - 1) + tile, BF16),

time: 81.9 us -> 81.9 us (level)
  no operation moved by 1% of the time
where the time goes in v7:
time: 81.9 us; the launch traced here: 81.4 us
  Pallas kernels  78.2 us (95%)
  local copies, waits for them, and re-layouts  1.9 us (2%)
  between operations  1.29 us (2%)
    pallas_call x1, Pallas kernels, per_device(): pl.pallas_call(functools.partial(kernel, 1.0 / math.sqrt(nodes)), out_sha...  78.2 us
    unnamed x3, local copies, waits for them, and re-layouts  1.9 us

profile of v7, /device:TPU:1, one launch (start us, length us, event | category | flops | bytes accessed | tf_op | source)
XLA Modules:
  0.0 81.4 jit_solution(8280330290961471071)
XLA Ops:
  1.3 78.2 %shard_map.94 = (bf16[128,256]{1,0:T(8,128)(2,1)S(1)}, bf16[128,128]{1,0:T(8,128)(2,1)S(1)}, f32[128,256]{1,0:T(8,128)S(1)}) custom-call(bf16[128,128]{1,0:T(8,128)(2,1)} %feat_hbm.1, bf16[128,256]{1,0:T(8,128)(2,1)} %weight_hbm.1, bf16[1,128,128,128]{3,2,1,0:T(8,128)(2,1)} %vals_hbm.1, s32[1,128]{1,0:T(1,128)} %row_hbm.1, s32[1,128]{1,0:T(1,128)} %col_hbm.1, ...), custom_call_target="tpu_custom_call" | custom-call | flops 1073741824 | bytes 4194304 | tf_op jit(solution)/shard_map/pallas_call | solution.py:310
  79.5 0.6 copy.13
  80.1 0.6 copy.14
  80.7 0.7 copy.15
